TPU v7x, 32 devices: a whole 2x2x4 slice. The times are simulated.
32 devices in a mesh: island: 4 (over y, x), fsdp: 8 (over z, core).
Axes of the slice: x: 2, y: 2, z: 4, core: 2. Of those that a mesh axis runs over, the one named last changes fastest.
Arguments:
- pseudo_grad: bfloat16 [4, 14336, 4096], P('island', 'fsdp'), may hold values from -110 to 110
- error_buffer: bfloat16 [4, 14336, 4096], P('island', 'fsdp'), may hold values from -3 to 3
- basis_init: float32 [4096, 64], replicated, may hold values from -6 to 6
- params: float32 [14336, 4096], P(('fsdp', 'island')), may hold values from -6 to 6
- momentum: float32 [14336, 4096], P(('fsdp', 'island')), may hold values from -6 to 6
Outputs:
- new_error: bfloat16 [4, 14336, 4096], P('island', 'fsdp')
- new_params: float32 [14336, 4096], P(('fsdp', 'island'))
- new_momentum: float32 [14336, 4096], P(('fsdp', 'island'))
All inputs are finite; a program needn't handle non-finite values.
Results may differ from a plain program's by a relative error of at most 0.0051.
Values sent between devices are 32-bit elements; how exact they have to be, the bound alone decides.
A program may use at most 192 MiB of HBM per device.

v0:
```python
import jax
import jax.numpy as jnp
from jax import lax
from jax.sharding import PartitionSpec as P

ITERS = 4


momentum_coef = 0.9
outer_rate = 0.7


def shards(pseudo_grad, error_buffer, basis_init, params, momentum):
    combined = (pseudo_grad[0].astype(jnp.float32) + error_buffer[0].astype(jnp.float32)).astype(
        jnp.bfloat16
    )
    quarter = params.shape[0]
    island_index = lax.axis_index("island")
    right_basis = basis_init
    for sweep in range(ITERS):
        partial_sketch = jnp.dot(
            combined,
            right_basis,
            precision=lax.Precision.HIGHEST,
            preferred_element_type=jnp.float32,
        )
        sketch = lax.psum(partial_sketch, "island")
        own_rows = lax.dynamic_slice_in_dim(sketch, island_index * quarter, quarter, 0)
        gram_part = jnp.dot(
            own_rows.T,
            own_rows,
            precision=lax.Precision.HIGHEST,
            preferred_element_type=jnp.float32,
        )
        projected, gram = lax.psum(
            (
                jnp.einsum(
                    "nd,nr->dr",
                    combined,
                    sketch,
                    precision=lax.Precision.HIGHEST,
                    preferred_element_type=jnp.float32,
                ),
                gram_part,
            ),
            ("island", "fsdp"),
        )
        factor = jnp.linalg.cholesky(gram)
        right_basis = lax.linalg.triangular_solve(
            factor, projected, left_side=False, lower=True, transpose_a=True
        )
    orthonormal = lax.linalg.triangular_solve(
        factor, sketch, left_side=False, lower=True, transpose_a=True
    )
    inverse_count = 1.0 / lax.axis_size("island")
    approx_full = (
        jnp.einsum(
            "nr,dr->nd",
            orthonormal,
            right_basis,
            precision=lax.Precision.HIGHEST,
            preferred_element_type=jnp.float32,
        )
        * inverse_count
    )
    approx = lax.dynamic_slice_in_dim(approx_full, island_index * quarter, quarter, 0)
    new_error = (combined.astype(jnp.float32) - approx_full).astype(jnp.bfloat16)[None]
    new_momentum = momentum_coef * momentum + approx
    new_params = params - outer_rate * (approx + momentum_coef * new_momentum)
    return (new_error, new_params, new_momentum)


def solution(mesh):
    placed = (
        P("island", "fsdp", None),
        P("island", "fsdp", None),
        P(),
        P(("fsdp", "island"), None),
        P(("fsdp", "island"), None),
    )
    return jax.shard_map(
        shards,
        mesh=mesh,
        in_specs=placed,
        out_specs=(
            P("island", "fsdp", None),
            P(("fsdp", "island"), None),
            P(("fsdp", "island"), None),
        ),
        check_vma=False,
    )
```

profile of v0, /device:TPU:0, one launch (start us, length us, event | category | flops | bytes accessed | tf_op | source)
XLA Modules:
  0.0 1136.0 jit_solution(16907774162942144549)
XLA Ops:
  7.2 12.5 %fusion = bf16[1792,4096]{1,0:T(8,128)(2,1)S(1)} fusion(bf16[1,1792,4096]{2,1,0:T(8,128)(2,1)} %param.9, bf16[1,1792,4096]{2,1,0:T(8,128)(2,1)} %param.8), kind=kLoop, calls=%fused_computation.3 | loop fusion | flops 29360128 | bytes 44040192 | tf_op jit(solution)/shard_map/convert_element_type | solution.py:14
  19.8 5.5 copy-done.2
  25.2 14.1 %fusion.32 = f32[1792,64]{0,1:T(8,128)} fusion(bf16[1792,4096]{1,0:T(8,128)(2,1)S(1)} %fusion, f32[4096,64]{0,1:T(8,128)S(1)} %copy-done), kind=kOutput, calls=%fused_computation.57 | convolution fusion | flops 5637144576 | bytes 16187392 | tf_op jit(solution)/shard_map/dot_general | solution.py:21
  39.4 47.5 %all-reduce.9.cloned.1.call-done = f32[1792,64]{0,1:T(8,128)} async-done(((f32[1792,64]{0,1:T(8,128)}), f32[1792,64]{0,1:T(8,128)}) %all-reduce.9.cloned.1.call-update) | async-done | bytes 458768 | tf_op jit(solution)/shard_map/psum | solution.py:27
  86.9 1.3 fusion.8
  88.2 39.7 %psum.85 = f32[64,64]{0,1:T(8,128)S(1)} all-reduce(f32[64,64]{0,1:T(8,128)S(1)} %fusion.8), channel_id=1, replica_groups=mesh['island'=4,'fsdp'=8] {'island','fsdp'}, use_global_device_ids=true, to_apply=%region_1.0 | all-reduce | flops 4096 | bytes 32768 | tf_op jit(solution)/shard_map/psum | solution.py:35
  128.0 19.6 %fusion.33 = f32[4096,64]{1,0:T(8,128)} fusion(bf16[1792,4096]{1,0:T(8,128)(2,1)} %copy-done.2, f32[1792,64]{0,1:T(8,128)} %all-reduce.9.cloned.1.call-done), kind=kOutput, calls=%fused_computation.58 | convolution fusion | flops 5637144576 | bytes 16187392 | tf_op jit(solution)/shard_map/nd,nr->dr/dot_general | solution.py:37
  147.9 5.8 cholesky.74
  153.8 0.6 compare_reduce_fusion.3
  154.5 0.7 fusion.10
  155.1 4.9 custom-call.12
  160.0 122.5 %all-reduce.11.cloned.1.call-done = f32[4096,64]{1,0:T(8,128)} async-done(((f32[4096,64]{1,0:T(8,128)}), f32[4096,64]{1,0:T(8,128)}) %all-reduce.11.cloned.1.call-update) | async-done | bytes 1048592 | tf_op jit(solution)/shard_map/psum | solution.py:35
  282.5 3.9 convolution_bitcast_fusion.3
  286.4 17.3 %fusion.34 = f32[1792,64]{0,1:T(8,128)} fusion(bf16[1792,4096]{1,0:T(8,128)(2,1)} %copy-done.2, f32[4096,64]{0,1:T(8,128)S(1)} %convolution_bitcast_fusion.3), kind=kOutput, calls=%fused_computation.59 | convolution fusion | flops 5637144576 | bytes 16187392 | tf_op jit(solution)/shard_map/dot_general | solution.py:21
  303.8 43.7 %all-reduce.13.cloned.1.call-done = f32[1792,64]{0,1:T(8,128)} async-done(((f32[1792,64]{0,1:T(8,128)}), f32[1792,64]{0,1:T(8,128)}) %all-reduce.13.cloned.1.call-update) | async-done | bytes 458768 | tf_op jit(solution)/shard_map/psum | solution.py:27
  347.5 1.3 fusion.6
  348.9 40.0 %psum.88 = f32[64,64]{0,1:T(8,128)S(1)} all-reduce(f32[64,64]{0,1:T(8,128)S(1)} %fusion.6), channel_id=1, replica_groups=mesh['island'=4,'fsdp'=8] {'island','fsdp'}, use_global_device_ids=true, to_apply=%region_6.9 | all-reduce | flops 4096 | bytes 32768 | tf_op jit(solution)/shard_map/psum | solution.py:35
  388.9 19.6 %fusion.35 = f32[4096,64]{1,0:T(8,128)} fusion(bf16[1792,4096]{1,0:T(8,128)(2,1)} %copy-done.2, f32[1792,64]{0,1:T(8,128)} %all-reduce.13.cloned.1.call-done), kind=kOutput, calls=%fused_computation.60 | convolution fusion | flops 5637144576 | bytes 16187392 | tf_op jit(solution)/shard_map/nd,nr->dr/dot_general | solution.py:37
  408.8 5.8 cholesky.85
  414.7 0.6 compare_reduce_fusion.2
  415.3 0.7 fusion.11
  416.0 4.9 custom-call.13
  420.9 122.6 %all-reduce.15.cloned.1.call-done = f32[4096,64]{1,0:T(8,128)} async-done(((f32[4096,64]{1,0:T(8,128)}), f32[4096,64]{1,0:T(8,128)}) %all-reduce.15.cloned.1.call-update) | async-done | bytes 1048592 | tf_op jit(solution)/shard_map/psum | solution.py:35
  543.4 3.9 convolution_bitcast_fusion.2
  547.3 17.3 %fusion.36 = f32[1792,64]{0,1:T(8,128)} fusion(bf16[1792,4096]{1,0:T(8,128)(2,1)} %copy-done.2, f32[4096,64]{0,1:T(8,128)S(1)} %convolution_bitcast_fusion.2), kind=kOutput, calls=%fused_computation.61 | convolution fusion | flops 5637144576 | bytes 16187392 | tf_op jit(solution)/shard_map/dot_general | solution.py:21
  564.7 43.7 %all-reduce.17.cloned.1.call-done = f32[1792,64]{0,1:T(8,128)} async-done(((f32[1792,64]{0,1:T(8,128)}), f32[1792,64]{0,1:T(8,128)}) %all-reduce.17.cloned.1.call-update) | async-done | bytes 458768 | tf_op jit(solution)/shard_map/psum | solution.py:27
  608.4 1.3 fusion.4
  609.8 39.7 %psum.91 = f32[64,64]{0,1:T(8,128)S(1)} all-reduce(f32[64,64]{0,1:T(8,128)S(1)} %fusion.4), channel_id=1, replica_groups=mesh['island'=4,'fsdp'=8] {'island','fsdp'}, use_global_device_ids=true, to_apply=%region_9.12 | all-reduce | flops 4096 | bytes 32768 | tf_op jit(solution)/shard_map/psum | solution.py:35
  649.6 19.6 %fusion.37 = f32[4096,64]{1,0:T(8,128)} fusion(bf16[1792,4096]{1,0:T(8,128)(2,1)} %copy-done.2, f32[1792,64]{0,1:T(8,128)} %all-reduce.17.cloned.1.call-done), kind=kOutput, calls=%fused_computation.62 | convolution fusion | flops 5637144576 | bytes 16187392 | tf_op jit(solution)/shard_map/nd,nr->dr/dot_general | solution.py:37
  669.5 5.8 cholesky.96
  676.0 0.7 fusion.12
  676.7 4.9 custom-call.14
  681.6 122.5 %all-reduce.19.cloned.1.call-done = f32[4096,64]{1,0:T(8,128)} async-done(((f32[4096,64]{1,0:T(8,128)}), f32[4096,64]{1,0:T(8,128)}) %all-reduce.19.cloned.1.call-update) | async-done | bytes 1048592 | tf_op jit(solution)/shard_map/psum | solution.py:35
  804.1 3.9 convolution_bitcast_fusion.1
  808.0 17.3 %fusion.38 = f32[1792,64]{0,1:T(8,128)} fusion(bf16[1792,4096]{1,0:T(8,128)(2,1)} %copy-done.2, f32[4096,64]{0,1:T(8,128)S(1)} %convolution_bitcast_fusion.1), kind=kOutput, calls=%fused_computation.63 | convolution fusion | flops 5637144576 | bytes 16187392 | tf_op jit(solution)/shard_map/dot_general | solution.py:21
  825.4 43.7 %all-reduce.21.cloned.1.call-done = f32[1792,64]{0,1:T(8,128)} async-done(((f32[1792,64]{0,1:T(8,128)}), f32[1792,64]{0,1:T(8,128)}) %all-reduce.21.cloned.1.call-update) | async-done | bytes 458768 | tf_op jit(solution)/shard_map/psum | solution.py:27
  869.1 1.4 fusion.2
  870.5 40.0 %psum.94 = f32[64,64]{0,1:T(8,128)S(1)} all-reduce(f32[64,64]{0,1:T(8,128)S(1)} %fusion.2), channel_id=1, replica_groups=mesh['island'=4,'fsdp'=8] {'island','fsdp'}, use_global_device_ids=true, to_apply=%region_12.15 | all-reduce | flops 4096 | bytes 32768 | tf_op jit(solution)/shard_map/psum | solution.py:35
  910.6 5.8 cholesky.107
  916.4 19.8 %fusion.39 = f32[4096,64]{1,0:T(8,128)} fusion(bf16[1792,4096]{1,0:T(8,128)(2,1)} %copy-done.2, f32[1792,64]{0,1:T(8,128)} %all-reduce.21.cloned.1.call-done), kind=kOutput, calls=%fused_computation.64 | convolution fusion | flops 5637144576 | bytes 16187392 | tf_op jit(solution)/shard_map/nd,nr->dr/dot_general | solution.py:37
  936.9 0.7 fusion.13
  937.5 4.9 custom-call.8
  942.4 1.6 fusion.15
  944.0 126.9 %all-reduce.23.cloned.1.call-done = f32[4096,64]{1,0:T(8,128)} async-done(((f32[4096,64]{1,0:T(8,128)}), f32[4096,64]{1,0:T(8,128)}) %all-reduce.23.cloned.1.call-update) | async-done | bytes 1048592 | tf_op jit(solution)/shard_map/psum | solution.py:35
  1071.0 4.1 convolution_bitcast_fusion
  1075.1 26.4 %convolution_multiply_fusion = f32[1792,4096]{1,0:T(8,128)} fusion(f32[1792,64]{1,0:T(8,128)S(1)} %fusion.15, f32[4096,64]{0,1:T(8,128)S(1)} %convolution_bitcast_fusion), kind=kOutput, calls=%fused_computation.2 | convolution fusion | flops 5644484608 | bytes 30867456 | tf_op jit(solution)/shard_map/nr,dr->nd/dot_general | solution.py:57
  1101.6 18.8 %fusion.1 = bf16[1,1792,4096]{2,1,0:T(8,128)(2,1)} fusion(f32[1792,4096]{1,0:T(8,128)} %convolution_multiply_fusion, bf16[1792,4096]{1,0:T(8,128)(2,1)S(1)} %bitcast.76), kind=kLoop, calls=%fused_computation.4 | loop fusion | flops 22020096 | bytes 58720256 | tf_op jit(solution)/shard_map/broadcast_in_dim | solution.py:67
  1120.4 8.6 multiply_subtract_fusion
  (56 shorter events, 2.9 us)
Async XLA Ops:
  7.2 18.1 %copy-start = (f32[4096,64]{0,1:T(8,128)S(1)}, f32[4096,64]{0,1:T(8,128)}, u32[]{:S(2)}) copy-start(f32[4096,64]{0,1:T(8,128)} %param.10) | copy-start | bytes 3145732
  7.2 79.7 %all-reduce.9.cloned.1.call-start = ((), (), s32[]{:S(2)}) async-start(), calls=%async_computation | async-start | bytes 917504 | tf_op jit(solution)/shard_map/psum | solution.py:27
  19.7 5.5 copy-start.2
  39.3 243.2 %all-reduce.11.cloned.1.call-start = ((), (), s32[]{:S(2)}) async-start(), calls=%async_computation.1 | async-start | bytes 4194304 | tf_op jit(solution)/shard_map/psum | solution.py:35
  147.6 199.9 %all-reduce.13.cloned.1.call-start = ((), (), s32[]{:S(2)}) async-start(), calls=%async_computation.2 | async-start | bytes 917504 | tf_op jit(solution)/shard_map/psum | solution.py:27
  303.8 239.6 %all-reduce.15.cloned.1.call-start = ((), (), s32[]{:S(2)}) async-start(), calls=%async_computation.3 | async-start | bytes 4194304 | tf_op jit(solution)/shard_map/psum | solution.py:35
  408.5 199.9 %all-reduce.17.cloned.1.call-start = ((), (), s32[]{:S(2)}) async-start(), calls=%async_computation.4 | async-start | bytes 917504 | tf_op jit(solution)/shard_map/psum | solution.py:27
  564.7 239.4 %all-reduce.19.cloned.1.call-start = ((), (), s32[]{:S(2)}) async-start(), calls=%async_computation.5 | async-start | bytes 4194304 | tf_op jit(solution)/shard_map/psum | solution.py:35
  669.2 199.9 %all-reduce.21.cloned.1.call-start = ((), (), s32[]{:S(2)}) async-start(), calls=%async_computation.6 | async-start | bytes 917504 | tf_op jit(solution)/shard_map/psum | solution.py:27
  825.3 245.6 %all-reduce.23.cloned.1.call-start = ((), (), s32[]{:S(2)}) async-start(), calls=%async_computation.7 | async-start | bytes 4194304 | tf_op jit(solution)/shard_map/psum | solution.py:35
  869.1 73.3 %copy-start.3 = (f32[1792,64]{0,1:T(8,128)S(1)}, f32[1792,64]{0,1:T(8,128)}, u32[]{:S(2)}) copy-start(f32[1792,64]{0,1:T(8,128)} %all-reduce.21.cloned.1.call-done) | copy-start | bytes 1376260
  1071.0 30.5 %slice-start = ((s8[14680064]{0:T(1024)(128)(4,1)}), s8[4194304]{0:T(1024)(128)(4,1)S(1)}, s32[]{:S(2)}) async-start(s8[14680064]{0:T(1024)(128)(4,1)} %bitcast.75), calls=%async_computation.8 | async-start | bytes 8388608
  1075.0 26.5 %slice-start.1 = ((s8[14680064]{0:T(1024)(128)(4,1)}), s8[4194304]{0:T(1024)(128)(4,1)S(1)}, s32[]{:S(2)}) async-start(s8[14680064]{0:T(1024)(128)(4,1)} %bitcast.75), calls=%async_computation.9 | async-start | bytes 8388608
  1075.0 26.5 %slice-start.2 = ((s8[14680064]{0:T(1024)(128)(4,1)}), s8[4194304]{0:T(1024)(128)(4,1)S(1)}, s32[]{:S(2)}) async-start(s8[14680064]{0:T(1024)(128)(4,1)} %bitcast.75), calls=%async_computation.10 | async-start | bytes 8388608
  1075.0 26.5 %slice-start.3 = ((s8[14680064]{0:T(1024)(128)(4,1)}), s8[2097152]{0:T(1024)(128)(4,1)S(1)}, s32[]{:S(2)}) async-start(s8[14680064]{0:T(1024)(128)(4,1)} %bitcast.75), calls=%async_computation.11 | async-start | bytes 4194304
  1075.0 45.3 %slice-start.4 = ((s8[7340032]{0:T(1024)(128)(4,1)}), s8[4194304]{0:T(1024)(128)(4,1)S(1)}, s32[]{:S(2)}) async-start(s8[7340032]{0:T(1024)(128)(4,1)} %bitcast.77), calls=%async_computation.12 | async-start | bytes 8388608
  1075.1 45.3 %slice-start.6 = ((s8[7340032]{0:T(1024)(128)(4,1)}), s8[4194304]{0:T(1024)(128)(4,1)S(1)}, s32[]{:S(2)}) async-start(s8[7340032]{0:T(1024)(128)(4,1)} %bitcast.79), calls=%async_computation.14 | async-start | bytes 8388608
  1101.5 18.8 %slice-start.5 = ((s8[7340032]{0:T(1024)(128)(4,1)}), s8[3145728]{0:T(1024)(128)(4,1)S(1)}, s32[]{:S(2)}) async-start(s8[7340032]{0:T(1024)(128)(4,1)} %bitcast.77), calls=%async_computation.13 | async-start | bytes 6291456
  1101.5 18.8 %slice-start.7 = ((s8[7340032]{0:T(1024)(128)(4,1)}), s8[3145728]{0:T(1024)(128)(4,1)S(1)}, s32[]{:S(2)}) async-start(s8[7340032]{0:T(1024)(128)(4,1)} %bitcast.79), calls=%async_computation.15 | async-start | bytes 6291456
  1101.6 27.4 %copy-start.1 = (f32[4096,64]{0,1:T(8,128)S(1)}, f32[4096,64]{0,1:T(8,128)}, u32[]{:S(2)}) copy-start(f32[4096,64]{0,1:T(8,128)} %param.10) | copy-start | bytes 3145732
Sparse Core Ops, SparseCore 0:
  39.4 47.3 all-reduce.8
  147.7 134.7 all-reduce.10
  303.9 43.5 all-reduce.12
  408.7 134.7 all-reduce.14
  564.8 43.5 all-reduce.16
  669.3 134.7 all-reduce.18
  825.5 43.5 all-reduce.20
  936.3 134.5 all-reduce.22
where the time goes:
time: 1140 us
  waiting for transfers between devices  673 us (59%)
  matrix products  194 us (17%)
  blocking collectives  159 us (14%)
  other arithmetic  88.2 us (8%)
  between operations  14.7 us (1%)
    psum x4, waiting for transfers between devices, shards(): lax.psum((jnp.einsum('nd,nr->dr', combined, sketch, precision=lax.Precisi...  494 us
    psum x4, waiting for transfers between devices, shards(): sketch = lax.psum(partial_sketch, 'island')  179 us
    psum x4, blocking collectives, shards(): lax.psum((jnp.einsum('nd,nr->dr', combined, sketch, precision=lax.Precisi...  159 us
    dot_general x4, matrix products, shards(): jnp.einsum('nd,nr->dr', combined, sketch, precision=lax.Precision.HIGHEST...  78.6 us
    dot_general x4, matrix products, shards(): jnp.dot(combined, right_basis, precision=lax.Precision.HIGHEST, preferred...  66.1 us
    dot_general x1, matrix products, shards(): jnp.einsum('nr,dr->nd', orthonormal, right_basis, precision=lax.Precision...  26.4 us
    another operation x12, other arithmetic, shards(): factor = jnp.linalg.cholesky(gram)  26.1 us
  transfers between devices with their start and end apart: 8, of which 8 were waited for; matrix products, arithmetic and copies ran while one was open for 4% of the time, Pallas kernels for 0%

commit v1 on v0

v1 whole, which is shorter than its diff:
```python
import functools

import jax
import jax.numpy as jnp
from jax import lax
from jax.experimental import pallas as pl
from jax.experimental.pallas import tpu as pltpu
from jax.sharding import PartitionSpec as P

ITERS = 4

momentum_coef = 0.9
outer_rate = 0.7

MESH = pl.DeviceIdType.MESH
F32 = jnp.float32
BF16 = jnp.bfloat16
HIGH = lax.Precision.HIGHEST


def split(value):
    high = value.astype(BF16)
    low = (value - high.astype(F32)).astype(BF16)
    return high, low


def bits_of(extent):
    return extent.bit_length() - 1


def tile_of(extent, want):
    return want if extent % want == 0 else extent


def partner_of(index, bit):
    stride = 1 << bit
    own = (index // stride) % 2
    return index + (1 - 2 * own) * stride, own


def power_kernel(
    islands,
    shards,
    grad_ref,
    error_ref,
    basis_ref,
    combined_out,
    left_out,
    right_out,
    combined,
    grad_stage,
    error_stage,
    basis_parts,
    sketch,
    sketch_in,
    sketch_parts,
    gram,
    gram_in,
    work,
    projected,
    core_in,
    held,
    first_in,
    first,
    second_in,
    second,
    line_in,
    first_all,
    held_all,
    projected_all,
    stage_sem,
    out_sem,
    send_sem,
    recv_sem,
):
    island = lax.axis_index("island")
    shard = lax.axis_index("fsdp")
    rows, wide = combined.shape
    rank = sketch.shape[0]
    half_rank, half_wide = rank // 2, wide // 2
    island_bits, shard_bits = bits_of(islands), bits_of(shards)

    def island_peer(bit):
        index, own = partner_of(island, bit)
        return (index, shard), own

    def shard_peer(bit):
        index, own = partner_of(shard, bit)
        return (island, index), own

    peers = [island_peer(b)[0] for b in range(island_bits)] + [shard_peer(b)[0] for b in range(shard_bits)]

    counter = [0]

    def send(src, dst, peer):
        number = counter[0]
        counter[0] += 1
        copy = pltpu.make_async_remote_copy(
            src_ref=src,
            dst_ref=dst,
            send_sem=send_sem.at[number],
            recv_sem=recv_sem.at[number],
            device_id=peer,
            device_id_type=MESH,
        )
        copy.start()
        return copy

    tile = tile_of(rows, 256)
    tiles = rows // tile

    def fetch(t, slot):
        span = pl.ds(pl.multiple_of(t * tile, tile), tile)
        return (
            pltpu.make_async_copy(grad_ref.at[0, span], grad_stage.at[slot], stage_sem.at[0, slot]),
            pltpu.make_async_copy(error_ref.at[0, span], error_stage.at[slot], stage_sem.at[1, slot]),
        )

    for copy in fetch(0, 0):
        copy.start()

    barrier = pltpu.get_barrier_semaphore()
    for peer in peers:
        pl.semaphore_signal(barrier, inc=1, device_id=peer, device_id_type=MESH)
    pl.semaphore_wait(barrier, len(peers))

    strip = tile_of(wide, 512)
    strips = wide // strip

    def strip_span(s):
        return pl.ds(pl.multiple_of(s * strip, strip), strip)

    @pl.loop(0, strips)
    def _(s):
        span = strip_span(s)
        high, low = split(basis_ref[:, span])
        basis_parts[0:rank, span] = high
        basis_parts[rank:, span] = low

    def sketch_tile(t):
        span = pl.ds(pl.multiple_of(t * tile, tile), tile)
        both = lax.dot_general(
            basis_parts[...], combined[span, :], (((1,), (1,)), ((), ())), preferred_element_type=F32
        )
        sketch[:, span] = both[0:rank] + both[rank:]

    @pl.loop(0, tiles)
    def _(t):
        slot = lax.rem(t, 2)

        @pl.when(t + 1 < tiles)
        def _():
            for copy in fetch(t + 1, 1 - slot):
                copy.start()

        for copy in fetch(t, slot):
            copy.wait()

        @pl.loop(0, tile // 16)
        def _(r):
            part = pl.ds(pl.multiple_of(r * 16, 16), 16)
            total = grad_stage[slot, part, :].astype(F32) + error_stage[slot, part, :].astype(F32)
            combined[pl.ds(pl.multiple_of(t * tile + r * 16, 16), 16), :] = total.astype(BF16)

        sketch_tile(t)

    keep = pltpu.make_async_copy(combined, combined_out, out_sem)
    keep.start()

    lane = lax.broadcasted_iota(jnp.int32, (rank, 2 * rank), 1)
    line = lax.broadcasted_iota(jnp.int32, (rank, 2 * rank), 0)

    def eliminate(begin, end):
        def step(j, carry):
            value = work[...]
            row = work[pl.ds(j, 1), :]
            column = jnp.sum(jnp.where(lane == j + rank, value, 0.0), axis=1, keepdims=True)
            pivot = jnp.sum(jnp.where(lane[0:1] == j + rank, row, 0.0), axis=1, keepdims=True)
            scale = jnp.where(line[:, 0:1] > j, column / pivot, 0.0)
            work[...] = value - scale * row
            return carry

        lax.fori_loop(begin, end, step, 0)

    stages = 2 + 2 * 2 + (shard_bits - 1)

    def iteration(sweep, carry):
        counter[0] = 0
        for s in range(island_bits):
            one = send(
                sketch.at[0:half_rank], sketch_in.at[s, 0:half_rank], island_peer(s)[0]
            )
            two = send(
                sketch.at[half_rank:rank], sketch_in.at[s, half_rank:rank], island_peer(island_bits - 1 - s)[0]
            )
            one.wait()
            two.wait()
            sketch[...] += sketch_in[s]
        high, low = split(sketch[...])
        sketch_parts[0:rank] = high
        sketch_parts[rank:] = low

        value = sketch[...]
        gram[...] = lax.dot_general(
            value,
            jnp.concatenate([value, value], axis=0),
            (((1,), (1,)), ((), ())),
            precision=HIGH,
            preferred_element_type=F32,
        )

        def project(begin, end):
            @pl.loop(begin, end)
            def _(s):
                span = strip_span(s)
                both = jnp.dot(sketch_parts[...], combined[:, span], preferred_element_type=F32)
                projected[:, span] = both[0:rank] + both[rank:]

        cuts = [strips * i // shard_bits for i in range(shard_bits + 1)]
        for s in range(shard_bits):
            copy = send(gram, gram_in.at[s], shard_peer(s)[0])
            project(cuts[s], cuts[s + 1])
            copy.wait()
            gram[...] += gram_in[s]
        work[...] = jnp.where(lane < rank, jnp.where(lane == line, 1.0, 0.0), gram[...])

        place = [0]

        def finish(*copies):
            begin = rank * place[0] // stages
            place[0] += 1
            eliminate(begin, rank * place[0] // stages)
            for copy in copies:
                copy.wait()

        core_peer, core = shard_peer(0)
        own = pl.ds(pl.multiple_of(core * half_rank, half_rank), half_rank)
        other = pl.ds(pl.multiple_of((1 - core) * half_rank, half_rank), half_rank)
        finish(send(projected.at[other], core_in, core_peer))
        held[...] = projected[own, :] + core_in[...]

        left, right = slice(0, half_wide), slice(half_wide, wide)
        peer_a, bit_a = island_peer(0)
        peer_b, bit_b = island_peer(1)
        quarter, eighth = half_rank // 2, half_rank // 4

        def part(index, size):
            return pl.ds(pl.multiple_of(index * size, size), size)

        finish(
            send(held.at[part(1 - bit_a, quarter), left], first_in.at[:, left], peer_a),
            send(held.at[part(1 - bit_b, quarter), right], first_in.at[:, right], peer_b),
        )
        first[:, left] = held[part(bit_a, quarter), left] + first_in[:, left]
        first[:, right] = held[part(bit_b, quarter), right] + first_in[:, right]
        finish(
            send(first.at[part(1 - bit_b, eighth), left], second_in.at[:, left], peer_b),
            send(first.at[part(1 - bit_a, eighth), right], second_in.at[:, right], peer_a),
        )
        second[:, left] = first[part(bit_b, eighth), left] + second_in[:, left]
        second[:, right] = first[part(bit_a, eighth), right] + second_in[:, right]
        for s in range(1, shard_bits):
            finish(send(second, line_in.at[s - 1], shard_peer(s)[0]))
            second[...] += line_in[s - 1]

        first_all[part(bit_b, eighth), left] = second[:, left]
        first_all[part(bit_a, eighth), right] = second[:, right]
        finish(
            send(second.at[:, left], first_all.at[part(bit_b, eighth), left], peer_b),
            send(second.at[:, right], first_all.at[part(bit_a, eighth), right], peer_a),
        )
        held_all[part(bit_a, quarter), left] = first_all[:, left]
        held_all[part(bit_b, quarter), right] = first_all[:, right]
        finish(
            send(first_all.at[:, left], held_all.at[part(bit_a, quarter), left], peer_a),
            send(first_all.at[:, right], held_all.at[part(bit_b, quarter), right], peer_b),
        )
        projected_all[own, :] = held_all[...]
        finish(send(held_all, projected_all.at[own], core_peer))

        value = work[...]
        diagonal = jnp.sum(jnp.where(lane == line + rank, value, 0.0), axis=1, keepdims=True)
        inverse = (value * (1.0 / jnp.sqrt(diagonal)))[:, 0:rank]

        @pl.when(sweep < ITERS - 1)
        def _():
            @pl.loop(0, strips)
            def _(s):
                span = strip_span(s)
                basis = jnp.dot(inverse, projected_all[:, span], precision=HIGH, preferred_element_type=F32)
                high, low = split(basis)
                basis_parts[0:rank, span] = high
                basis_parts[rank:, span] = low

            @pl.loop(0, tiles)
            def _(t):
                sketch_tile(t)

        @pl.when(sweep == ITERS - 1)
        def _():
            @pl.loop(0, strips)
            def _(s):
                span = strip_span(s)
                basis = jnp.dot(inverse, projected_all[:, span], precision=HIGH, preferred_element_type=F32)
                high, low = split(basis * (1.0 / islands))
                right_out[0:rank, span] = high
                right_out[rank : 2 * rank, span] = low
                right_out[2 * rank :, span] = high

            orthonormal = jnp.dot(inverse, sketch[...], precision=HIGH, preferred_element_type=F32)
            high, low = split(orthonormal)
            left_out[0:rank, :] = high
            left_out[rank : 2 * rank, :] = high
            left_out[2 * rank :, :] = low

        return carry

    lax.fori_loop(0, ITERS, iteration, 0)
    keep.wait()


def outer_kernel(combined_ref, left_ref, own_left_ref, right_ref, params_ref, momentum_ref, error_out, params_out, momentum_out):
    approx = jnp.dot(left_ref[...], right_ref[...], preferred_element_type=F32)
    error_out[0] = (combined_ref[...].astype(F32) - approx).astype(BF16)
    own = jnp.dot(own_left_ref[0], right_ref[...], preferred_element_type=F32)
    new_momentum = momentum_coef * momentum_ref[...] + own
    momentum_out[...] = new_momentum
    params_out[...] = params_ref[...] - outer_rate * (own + momentum_coef * new_momentum)


def steps_of(rows, quarter):
    for steps in (28, 14, 7, 4, 2):
        if rows % (16 * steps) == 0 and quarter % (8 * steps) == 0:
            return steps
    return 1


def shards(islands, shard_count, pseudo_grad, error_buffer, basis_init, params, momentum):
    _, rows, wide = pseudo_grad.shape
    rank = basis_init.shape[1]
    quarter = params.shape[0]
    half, tile = rank // 2, tile_of(rows, 256)
    island_bits, shard_bits = bits_of(islands), bits_of(shard_count)
    sends = 2 * island_bits + shard_bits + 2 + 2 * 4 + (shard_bits - 1)
    vmem = pl.BlockSpec(memory_space=pltpu.VMEM)
    hbm = pl.BlockSpec(memory_space=pl.ANY)
    combined, left, right = pl.pallas_call(
        functools.partial(power_kernel, islands, shard_count),
        out_shape=(
            jax.ShapeDtypeStruct((rows, wide), BF16),
            jax.ShapeDtypeStruct((3 * rank, rows), BF16),
            jax.ShapeDtypeStruct((3 * rank, wide), BF16),
        ),
        in_specs=[hbm, hbm, vmem],
        out_specs=(hbm, vmem, vmem),
        scratch_shapes=[
            pltpu.VMEM((rows, wide), BF16),
            pltpu.VMEM((2, tile, wide), BF16),
            pltpu.VMEM((2, tile, wide), BF16),
            pltpu.VMEM((2 * rank, wide), BF16),
            pltpu.VMEM((rank, rows), F32),
            pltpu.VMEM((island_bits, rank, rows), F32),
            pltpu.VMEM((2 * rank, rows), BF16),
            pltpu.VMEM((rank, 2 * rank), F32),
            pltpu.VMEM((shard_bits, rank, 2 * rank), F32),
            pltpu.VMEM((rank, 2 * rank), F32),
            pltpu.VMEM((rank, wide), F32),
            pltpu.VMEM((half, wide), F32),
            pltpu.VMEM((half, wide), F32),
            pltpu.VMEM((half // 2, wide), F32),
            pltpu.VMEM((half // 2, wide), F32),
            pltpu.VMEM((half // 4, wide), F32),
            pltpu.VMEM((half // 4, wide), F32),
            pltpu.VMEM((max(shard_bits - 1, 1), half // 4, wide), F32),
            pltpu.VMEM((half // 2, wide), F32),
            pltpu.VMEM((half, wide), F32),
            pltpu.VMEM((rank, wide), F32),
            pltpu.SemaphoreType.DMA((2, 2)),
            pltpu.SemaphoreType.DMA,
            pltpu.SemaphoreType.DMA((sends,)),
            pltpu.SemaphoreType.DMA((sends,)),
        ],
        compiler_params=pltpu.CompilerParams(
            collective_id=0, has_side_effects=True, vmem_limit_bytes=56 * 1024 * 1024
        ),
        name="power_iterations",
    )(pseudo_grad, error_buffer, basis_init.T)

    left = left.T
    steps = steps_of(rows, quarter)
    own_left = lax.dynamic_slice_in_dim(left, lax.axis_index("island") * quarter, quarter, 0)
    own_left = own_left.reshape(steps, quarter // steps, 3 * rank)
    tall, short = rows // steps, quarter // steps
    new_error, new_params, new_momentum = pl.pallas_call(
        outer_kernel,
        grid=(steps,),
        out_shape=(
            jax.ShapeDtypeStruct((1, rows, wide), BF16),
            jax.ShapeDtypeStruct((quarter, wide), F32),
            jax.ShapeDtypeStruct((quarter, wide), F32),
        ),
        in_specs=[
            pl.BlockSpec((tall, wide), lambda i: (i, 0)),
            pl.BlockSpec((tall, 3 * rank), lambda i: (i, 0)),
            pl.BlockSpec((1, short, 3 * rank), lambda i: (i, 0, 0)),
            pl.BlockSpec((3 * rank, wide), lambda i: (0, 0)),
            pl.BlockSpec((short, wide), lambda i: (i, 0)),
            pl.BlockSpec((short, wide), lambda i: (i, 0)),
        ],
        out_specs=(
            pl.BlockSpec((1, tall, wide), lambda i: (0, i, 0)),
            pl.BlockSpec((short, wide), lambda i: (i, 0)),
            pl.BlockSpec((short, wide), lambda i: (i, 0)),
        ),
        compiler_params=pltpu.CompilerParams(vmem_limit_bytes=48 * 1024 * 1024),
        name="outer_step",
    )(combined, left, own_left, right, params, momentum)
    return (new_error, new_params, new_momentum)


def solution(mesh):
    placed = (
        P("island", "fsdp", None),
        P("island", "fsdp", None),
        P(),
        P(("fsdp", "island"), None),
        P(("fsdp", "island"), None),
    )
    return jax.shard_map(
        functools.partial(shards, mesh.shape["island"], mesh.shape["fsdp"]),
        mesh=mesh,
        in_specs=placed,
        out_specs=(
            P("island", "fsdp", None),
            P(("fsdp", "island"), None),
            P(("fsdp", "island"), None),
        ),
        check_vma=False,
    )
```

time: 1140 us -> 288 us (0.25)
  waiting for transfers between devices: 673 us -> 0 us
  Pallas kernels: 0 us -> 282 us
  matrix products: 194 us -> 0 us
  blocking collectives: 159 us -> 0 us
  other arithmetic: 88.2 us -> 0 us
  between operations: 14.7 us -> 0.68 us
    psum x8 -> x0, waiting for transfers between devices: 673 us -> none  [the longest x4 494 us: shards(): lax.psum((jnp.einsum('nd,nr->dr', combined, sketch, precision=lax.Precisi...]
    pallas_call x0 -> x2, Pallas kernels: none -> 282 us  [the longest x1 251 us: shards(): pl.pallas_call(functools.partial(power_kernel, islands, shard_count), out...]
    dot_general x13 -> x0, matrix products: 177 us -> none  [the longest x4 78.6 us: shards(): jnp.einsum('nd,nr->dr', combined, sketch, precision=lax.Precision.HIGHEST...]
    psum x4 -> x0, blocking collectives: 159 us -> none  [shards(): lax.psum((jnp.einsum('nd,nr->dr', combined, sketch, precision=lax.Precisi...]
    another operation x20 -> x0, other arithmetic: 48.3 us -> none  [the longest x12 26.1 us: shards(): factor = jnp.linalg.cholesky(gram)]
    broadcast_in_dim x1 -> x0, other arithmetic: 18.8 us -> none  [shards(): (combined.astype(jnp.float32) - approx_full).astype(jnp.bfloat16)[None]]
    another operation x5 -> x0, matrix products: 17.4 us -> none  [the longest x4 15.8 us: shards(): lax.linalg.triangular_solve(factor, projected, left_side=False, lower=Tru...]
    convert_element_type x1 -> x0, other arithmetic: 12.5 us -> none  [shards(): (pseudo_grad[0].astype(jnp.float32) + error_buffer[0].astype(jnp.float32)...]
  transfers between devices with their start and end apart: 8 -> 0, of which waited for: 8 -> 0; matrix products, arithmetic and copies ran while one was open for 4% -> 0% of each run, Pallas kernels for 0% -> 0%
where the time goes in v1:
time: 288 us; the launch traced here: 287 us
  Pallas kernels  282 us (98%)
  local copies, waits for them, and re-layouts  4.03 us (1%)
    pallas_call x1, Pallas kernels, shards(): pl.pallas_call(functools.partial(power_kernel, islands, shard_count), out...  251 us
    pallas_call x1, Pallas kernels, shards(): pl.pallas_call(outer_kernel, grid=(steps,), out_shape=(jax.ShapeDtypeStru...  31.2 us

profile of v1, /device:TPU:0, one launch (start us, length us, event | category | flops | bytes accessed | tf_op | source)
XLA Modules:
  0.0 286.8 jit_solution(916536347856363962)
XLA Ops:
  0.6 250.9 %power_iterations.1 = (bf16[1792,4096]{1,0:T(8,128)(2,1)}, bf16[192,1792]{1,0:T(8,128)(2,1)}, bf16[192,4096]{1,0:T(8,128)(2,1)}) custom-call(bf16[1,1792,4096]{2,1,0:T(8,128)(2,1)} %grad_ref.1, bf16[1,1792,4096]{2,1,0:T(8,128)(2,1)} %error_ref.1, f32[64,4096]{1,0:T(8,128)} %bitcast.7), custom_call_target="tpu_custom_call" | custom-call | tf_op jit(solution)/shard_map/power_iterations/pallas_call | solution.py:347
  251.5 1.1 dynamic-slice_bitcast_fusion
  252.6 0.1 copy.9
  252.8 1.4 copy.8
  254.2 0.0 copy-start
  254.2 1.4 copy-done
  255.6 31.2 %outer_step.1 = (bf16[1,1792,4096]{2,1,0:T(8,128)(2,1)}, f32[448,4096]{1,0:T(8,128)}, f32[448,4096]{1,0:T(8,128)}) custom-call(bf16[1792,4096]{1,0:T(8,128)(2,1)} %get-tuple-element.6.combined_ref, bf16[1792,192]{1,0:T(8,128)(2,1)S(1)} %bitcast.5, bf16[28,16,192]{2,1,0:T(8,128)(2,1)S(1)} %bitcast.6, bf16[192,4096]{1,0:T(8,128)(2,1)S(1)} %copy-done, ...), custom_call_target="tpu_custom_call" | custom-call | tf_op jit(solution)/shard_map/outer_step/pallas_call | solution.py:394
Async XLA Ops:
  254.2 1.4 copy-start

commit v2 on v1

v2 whole, which is shorter than its diff:
```python
import functools

import jax
import jax.numpy as jnp
from jax import lax
from jax.experimental import pallas as pl
from jax.experimental.pallas import tpu as pltpu
from jax.sharding import PartitionSpec as P

ITERS = 4

momentum_coef = 0.9
outer_rate = 0.7

MESH = pl.DeviceIdType.MESH
F32 = jnp.float32
BF16 = jnp.bfloat16
HIGH = lax.Precision.HIGHEST


def split(value):
    high = value.astype(BF16)
    low = (value - high.astype(F32)).astype(BF16)
    return high, low


def bits_of(extent):
    return extent.bit_length() - 1


def tile_of(extent, want):
    return want if extent % want == 0 else extent


def partner_of(index, bit):
    stride = 1 << bit
    own = (index // stride) % 2
    return index + (1 - 2 * own) * stride, own


def power_kernel(
    islands,
    shards,
    grad_ref,
    error_ref,
    basis_ref,
    combined_out,
    left_out,
    right_out,
    combined,
    grad_stage,
    error_stage,
    basis_parts,
    sketch,
    sketch_in,
    sketch_parts,
    gram,
    gram_in,
    work,
    projected,
    core_in,
    held,
    first_in,
    first,
    second_in,
    second,
    line_in,
    second_all,
    first_all,
    held_all,
    projected_all,
    stage_sem,
    out_sem,
    send_sem,
    recv_sem,
):
    island = lax.axis_index("island")
    shard = lax.axis_index("fsdp")
    rows, wide = combined.shape
    rank = sketch.shape[0]
    half_rank = rank // 2
    island_bits, shard_bits = bits_of(islands), bits_of(shards)

    def island_peer(bit):
        index, own = partner_of(island, bit)
        return (index, shard), own

    def shard_peer(bit):
        index, own = partner_of(shard, bit)
        return (island, index), own

    peers = [island_peer(b)[0] for b in range(island_bits)] + [shard_peer(b)[0] for b in range(shard_bits)]

    counter = [0]

    def send(src, dst, peer):
        number = counter[0]
        counter[0] += 1
        copy = pltpu.make_async_remote_copy(
            src_ref=src,
            dst_ref=dst,
            send_sem=send_sem.at[number],
            recv_sem=recv_sem.at[number],
            device_id=peer,
            device_id_type=MESH,
        )
        copy.start()
        return copy

    tile = tile_of(rows, 256)
    tiles = rows // tile

    def fetch(t, slot):
        span = pl.ds(pl.multiple_of(t * tile, tile), tile)
        return (
            pltpu.make_async_copy(grad_ref.at[0, span], grad_stage.at[slot], stage_sem.at[0, slot]),
            pltpu.make_async_copy(error_ref.at[0, span], error_stage.at[slot], stage_sem.at[1, slot]),
        )

    for copy in fetch(0, 0):
        copy.start()

    barrier = pltpu.get_barrier_semaphore()
    for peer in peers:
        pl.semaphore_signal(barrier, inc=1, device_id=peer, device_id_type=MESH)
    pl.semaphore_wait(barrier, len(peers))

    strip = tile_of(wide, 512)
    strips = wide // strip

    def strip_span(s):
        return pl.ds(pl.multiple_of(s * strip, strip), strip)

    @pl.loop(0, strips)
    def _(s):
        span = strip_span(s)
        high, low = split(basis_ref[:, span])
        basis_parts[0:rank, span] = high
        basis_parts[rank:, span] = low

    cut = (tiles + 1) // 2
    row_chunks = [(0, cut), (cut, tiles)] if tiles > 1 else [(0, 1)]
    row_spans = [slice(begin * tile, end * tile) for begin, end in row_chunks]
    chunk_strips = [(c * strips // 2, (c + 1) * strips // 2) for c in range(2)]
    columns = [slice(begin * strip, end * strip) for begin, end in chunk_strips]

    def tile_span(t):
        return pl.ds(pl.multiple_of(t * tile, tile), tile)

    def sketch_part(t, cols):
        both = lax.dot_general(
            basis_parts[:, cols],
            combined[tile_span(t), cols],
            (((1,), (1,)), ((), ())),
            preferred_element_type=F32,
        )
        return both[0:rank] + both[rank:]

    def stream(begin, end):
        @pl.loop(begin, end)
        def _(t):
            slot = lax.rem(t, 2)

            @pl.when(t + 1 < tiles)
            def _():
                for copy in fetch(t + 1, 1 - slot):
                    copy.start()

            for copy in fetch(t, slot):
                copy.wait()

            @pl.loop(0, tile // 16)
            def _(r):
                part = pl.ds(pl.multiple_of(r * 16, 16), 16)
                total = grad_stage[slot, part, :].astype(F32) + error_stage[slot, part, :].astype(F32)
                combined[pl.ds(pl.multiple_of(t * tile + r * 16, 16), 16), :] = total.astype(BF16)

            sketch[:, tile_span(t)] = sketch_part(t, slice(0, wide))

    lane = lax.broadcasted_iota(jnp.int32, (rank, 2 * rank), 1)
    line = lax.broadcasted_iota(jnp.int32, (rank, 2 * rank), 0)

    def eliminate(begin, end):
        def step(j, carry):
            value = work[...]
            row = work[pl.ds(j, 1), :]
            column = jnp.sum(jnp.where(lane == j + rank, value, 0.0), axis=1, keepdims=True)
            pivot = jnp.sum(jnp.where(lane[0:1] == j + rank, row, 0.0), axis=1, keepdims=True)
            scale = jnp.where(line[:, 0:1] > j, column / pivot, 0.0)
            work[...] = value - scale * row
            return carry

        lax.fori_loop(begin, end, step, 0)

    core_peer, core = shard_peer(0)
    peer_a, bit_a = island_peer(0)
    peer_b, bit_b = island_peer(1)
    quarter, eighth = half_rank // 2, half_rank // 4

    def part(index, size):
        return pl.ds(pl.multiple_of(index * size, size), size)

    def sketch_flow(r):
        span = row_spans[r]
        upper, lower = slice(0, half_rank), slice(half_rank, rank)
        for s in range(island_bits):
            copies = (
                send(sketch.at[upper, span], sketch_in.at[s, upper, span], island_peer(s)[0]),
                send(sketch.at[lower, span], sketch_in.at[s, lower, span], island_peer(island_bits - 1 - s)[0]),
            )
            yield
            for copy in copies:
                copy.wait()
            sketch[:, span] += sketch_in[s, :, span]
        high, low = split(sketch[:, span])
        sketch_parts[0:rank, span] = high
        sketch_parts[rank:, span] = low

    def gram_flow():
        for s in range(shard_bits):
            copy = send(gram, gram_in.at[s], shard_peer(s)[0])
            yield
            copy.wait()
            gram[...] += gram_in[s]

    def factor_flow(c):
        cols = columns[c]
        middle = (cols.start + cols.stop) // 2
        left, right = slice(cols.start, middle), slice(middle, cols.stop)
        own, other = part(core, half_rank), part(1 - core, half_rank)

        copy = send(projected.at[other, cols], core_in.at[:, cols], core_peer)
        yield
        copy.wait()
        held[:, cols] = projected[own, cols] + core_in[:, cols]

        copies = (
            send(held.at[part(1 - bit_a, quarter), left], first_in.at[:, left], peer_a),
            send(held.at[part(1 - bit_b, quarter), right], first_in.at[:, right], peer_b),
        )
        yield
        for copy in copies:
            copy.wait()
        first[:, left] = held[part(bit_a, quarter), left] + first_in[:, left]
        first[:, right] = held[part(bit_b, quarter), right] + first_in[:, right]

        copies = (
            send(first.at[part(1 - bit_b, eighth), left], second_in.at[:, left], peer_b),
            send(first.at[part(1 - bit_a, eighth), right], second_in.at[:, right], peer_a),
        )
        yield
        for copy in copies:
            copy.wait()
        second[:, left] = first[part(bit_b, eighth), left] + second_in[:, left]
        second[:, right] = first[part(bit_a, eighth), right] + second_in[:, right]

        if shard_bits > 1:
            size = middle - cols.start
            near, bit = shard_peer(1)
            kept = pl.ds(pl.multiple_of(cols.start + bit * size, size), size)
            given = pl.ds(pl.multiple_of(cols.start + (1 - bit) * size, size), size)
            copy = send(second.at[:, given], line_in.at[0, :, given], near)
            yield
            copy.wait()
            second[:, kept] += line_in[0, :, kept]
            for s in range(2, shard_bits):
                copy = send(second.at[:, kept], line_in.at[s - 1, :, kept], shard_peer(s)[0])
                yield
                copy.wait()
                second[:, kept] += line_in[s - 1, :, kept]
            second_all[:, kept] = second[:, kept]
            copy = send(second.at[:, kept], second_all.at[:, kept], near)
            yield
            copy.wait()
        else:
            second_all[:, cols] = second[:, cols]

        first_all[part(bit_b, eighth), left] = second_all[:, left]
        first_all[part(bit_a, eighth), right] = second_all[:, right]
        copies = (
            send(second_all.at[:, left], first_all.at[part(bit_b, eighth), left], peer_b),
            send(second_all.at[:, right], first_all.at[part(bit_a, eighth), right], peer_a),
        )
        yield
        for copy in copies:
            copy.wait()

        held_all[part(bit_a, quarter), left] = first_all[:, left]
        held_all[part(bit_b, quarter), right] = first_all[:, right]
        copies = (
            send(first_all.at[:, left], held_all.at[part(bit_a, quarter), left], peer_a),
            send(first_all.at[:, right], held_all.at[part(bit_b, quarter), right], peer_b),
        )
        yield
        for copy in copies:
            copy.wait()

        projected_all[own, cols] = held_all[:, cols]
        copy = send(held_all.at[:, cols], projected_all.at[own, cols], core_peer)
        yield
        copy.wait()

    def resume(flow):
        return next(flow, True) is None

    def project(r, c):
        @pl.loop(*chunk_strips[c])
        def _(s):
            span = strip_span(s)
            both = jnp.dot(sketch_parts[:, row_spans[r]], combined[row_spans[r], span], preferred_element_type=F32)
            total = both[0:rank] + both[rank:]
            projected[:, span] = total if r == 0 else projected[:, span] + total

    def iteration(sweep, carry):
        counter[0] = 0
        flows = []
        for r, (begin, end) in enumerate(row_chunks):

            @pl.when(sweep == 0)
            def _():
                stream(begin, end)

            @pl.when(sweep > 0)
            def _():
                @pl.loop(begin, end)
                def _(t):
                    sketch[:, tile_span(t)] += sketch_part(t, columns[1])

            flows.append(sketch_flow(r))
            resume(flows[r])

        @pl.when(sweep == 0)
        def _():
            keep.start()

        for s in range(1, island_bits):
            for flow in flows:
                resume(flow)
        last = len(flows) - 1
        for r, flow in enumerate(flows):
            resume(flow)
            if r < last:
                project(r, 0)
                project(r, 1)

        value = sketch[...]
        gram[...] = lax.dot_general(
            value,
            jnp.concatenate([value, value], axis=0),
            (((1,), (1,)), ((), ())),
            precision=HIGH,
            preferred_element_type=F32,
        )
        grams = gram_flow()
        resume(grams)
        halves = [factor_flow(0), factor_flow(1)]
        project(last, 0)
        resume(halves[0])
        more = resume(grams)
        project(last, 1)
        resume(halves[1])
        at = 0
        while more:
            more = resume(grams)
            if at < 2:
                resume(halves[at])
                at += 1
        while at < 2:
            resume(halves[at])
            at += 1
        work[...] = jnp.where(lane < rank, jnp.where(lane == line, 1.0, 0.0), gram[...])

        left_stages = 6 + (shard_bits - 1 if shard_bits > 1 else -1)
        slots = 2 * left_stages - 1
        place = 0
        more = True
        while more:
            for half in halves:
                if place < slots:
                    eliminate(rank * place // slots, rank * (place + 1) // slots)
                place += 1
                more = resume(half)
                if not more:
                    break
        if place < slots:
            eliminate(rank * place // slots, rank)
        inverse = inverse_factor()
        gathered(sweep, inverse, 0)

        @pl.when(sweep < ITERS - 1)
        def _():
            @pl.loop(0, tiles)
            def _(t):
                sketch[:, tile_span(t)] = sketch_part(t, columns[0])

        @pl.when(sweep == ITERS - 1)
        def _():
            orthonormal = jnp.dot(inverse, sketch[...], precision=HIGH, preferred_element_type=F32)
            high, low = split(orthonormal)
            left_out[0:rank, :] = high
            left_out[rank : 2 * rank, :] = high
            left_out[2 * rank :, :] = low

        while resume(halves[1]):
            pass
        gathered(sweep, inverse, 1)
        return carry

    def inverse_factor():
        value = work[...]
        diagonal = jnp.sum(jnp.where(lane == line + rank, value, 0.0), axis=1, keepdims=True)
        return (value * (1.0 / jnp.sqrt(diagonal)))[:, 0:rank]

    def gathered(sweep, inverse, c):
        @pl.loop(*chunk_strips[c])
        def _(s):
            span = strip_span(s)
            basis = jnp.dot(inverse, projected_all[:, span], precision=HIGH, preferred_element_type=F32)

            @pl.when(sweep < ITERS - 1)
            def _():
                high, low = split(basis)
                basis_parts[0:rank, span] = high
                basis_parts[rank:, span] = low

            @pl.when(sweep == ITERS - 1)
            def _():
                high, low = split(basis * (1.0 / islands))
                right_out[0:rank, span] = high
                right_out[rank : 2 * rank, span] = low
                right_out[2 * rank :, span] = high

    keep = pltpu.make_async_copy(combined, combined_out, out_sem)
    lax.fori_loop(0, ITERS, iteration, 0)
    keep.wait()


def outer_kernel(combined_ref, left_ref, right_ref, params_ref, momentum_ref, error_out, params_out, momentum_out):
    tall = combined_ref.shape[0]
    approx = jnp.dot(left_ref[0], right_ref[...], preferred_element_type=F32)
    error_out[0] = (combined_ref[...].astype(F32) - approx[0:tall]).astype(BF16)
    own = approx[tall:]
    new_momentum = momentum_coef * momentum_ref[...] + own
    momentum_out[...] = new_momentum
    params_out[...] = params_ref[...] - outer_rate * (own + momentum_coef * new_momentum)


def steps_of(rows, quarter):
    for steps in (14, 7, 4, 2):
        if rows % (16 * steps) == 0 and quarter % (8 * steps) == 0:
            return steps
    return 1


def shards(islands, shard_count, pseudo_grad, error_buffer, basis_init, params, momentum):
    _, rows, wide = pseudo_grad.shape
    rank = basis_init.shape[1]
    quarter = params.shape[0]
    half, tile = rank // 2, tile_of(rows, 256)
    island_bits, shard_bits = bits_of(islands), bits_of(shard_count)
    sends = 4 * island_bits + shard_bits + 2 * (10 + shard_bits)
    vmem = pl.BlockSpec(memory_space=pltpu.VMEM)
    hbm = pl.BlockSpec(memory_space=pl.ANY)
    combined, left, right = pl.pallas_call(
        functools.partial(power_kernel, islands, shard_count),
        out_shape=(
            jax.ShapeDtypeStruct((rows, wide), BF16),
            jax.ShapeDtypeStruct((3 * rank, rows), BF16),
            jax.ShapeDtypeStruct((3 * rank, wide), BF16),
        ),
        in_specs=[hbm, hbm, vmem],
        out_specs=(hbm, vmem, vmem),
        scratch_shapes=[
            pltpu.VMEM((rows, wide), BF16),
            pltpu.VMEM((2, tile, wide), BF16),
            pltpu.VMEM((2, tile, wide), BF16),
            pltpu.VMEM((2 * rank, wide), BF16),
            pltpu.VMEM((rank, rows), F32),
            pltpu.VMEM((island_bits, rank, rows), F32),
            pltpu.VMEM((2 * rank, rows), BF16),
            pltpu.VMEM((rank, 2 * rank), F32),
            pltpu.VMEM((shard_bits, rank, 2 * rank), F32),
            pltpu.VMEM((rank, 2 * rank), F32),
            pltpu.VMEM((rank, wide), F32),
            pltpu.VMEM((half, wide), F32),
            pltpu.VMEM((half, wide), F32),
            pltpu.VMEM((half // 2, wide), F32),
            pltpu.VMEM((half // 2, wide), F32),
            pltpu.VMEM((half // 4, wide), F32),
            pltpu.VMEM((half // 4, wide), F32),
            pltpu.VMEM((max(shard_bits - 1, 1), half // 4, wide), F32),
            pltpu.VMEM((half // 4, wide), F32),
            pltpu.VMEM((half // 2, wide), F32),
            pltpu.VMEM((half, wide), F32),
            pltpu.VMEM((rank, wide), F32),
            pltpu.SemaphoreType.DMA((2, 2)),
            pltpu.SemaphoreType.DMA,
            pltpu.SemaphoreType.DMA((sends,)),
            pltpu.SemaphoreType.DMA((sends,)),
        ],
        compiler_params=pltpu.CompilerParams(
            collective_id=0, has_side_effects=True, vmem_limit_bytes=56 * 1024 * 1024
        ),
        name="power_iterations",
    )(pseudo_grad, error_buffer, basis_init.T)

    left = left.T
    steps = steps_of(rows, quarter)
    own_left = lax.dynamic_slice_in_dim(left, lax.axis_index("island") * quarter, quarter, 0)
    tall, short = rows // steps, quarter // steps
    left = jnp.concatenate(
        [left.reshape(steps, tall, 3 * rank), own_left.reshape(steps, short, 3 * rank)], axis=1
    )
    new_error, new_params, new_momentum = pl.pallas_call(
        outer_kernel,
        grid=(steps,),
        out_shape=(
            jax.ShapeDtypeStruct((1, rows, wide), BF16),
            jax.ShapeDtypeStruct((quarter, wide), F32),
            jax.ShapeDtypeStruct((quarter, wide), F32),
        ),
        in_specs=[
            pl.BlockSpec((tall, wide), lambda i: (i, 0)),
            pl.BlockSpec((1, tall + short, 3 * rank), lambda i: (i, 0, 0)),
            pl.BlockSpec((3 * rank, wide), lambda i: (0, 0)),
            pl.BlockSpec((short, wide), lambda i: (i, 0)),
            pl.BlockSpec((short, wide), lambda i: (i, 0)),
        ],
        out_specs=(
            pl.BlockSpec((1, tall, wide), lambda i: (0, i, 0)),
            pl.BlockSpec((short, wide), lambda i: (i, 0)),
            pl.BlockSpec((short, wide), lambda i: (i, 0)),
        ),
        compiler_params=pltpu.CompilerParams(vmem_limit_bytes=48 * 1024 * 1024),
        name="outer_step",
    )(combined, left, right, params, momentum)
    return (new_error, new_params, new_momentum)


def solution(mesh):
    placed = (
        P("island", "fsdp", None),
        P("island", "fsdp", None),
        P(),
        P(("fsdp", "island"), None),
        P(("fsdp", "island"), None),
    )
    return jax.shard_map(
        functools.partial(shards, mesh.shape["island"], mesh.shape["fsdp"]),
        mesh=mesh,
        in_specs=placed,
        out_specs=(
            P("island", "fsdp", None),
            P(("fsdp", "island"), None),
            P(("fsdp", "island"), None),
        ),
        check_vma=False,
    )
```

time: 288 us -> 249 us (0.86)
  Pallas kernels: 282 us -> 243 us
    pallas_call x1, Pallas kernels: 251 us -> 218 us  [shards(): pl.pallas_call(functools.partial(power_kernel, islands, shard_count), out...]
    pallas_call x1, Pallas kernels: 31.2 us -> 25.4 us  [shards(): pl.pallas_call(outer_kernel, grid=(steps,), out_shape=(jax.ShapeDtypeStru...]
where the time goes in v2:
time: 249 us; the launch traced here: 248 us
  Pallas kernels  243 us (98%)
  local copies, waits for them, and re-layouts  4.03 us (2%)
    pallas_call x1, Pallas kernels, shards(): pl.pallas_call(functools.partial(power_kernel, islands, shard_count), out...  218 us
    pallas_call x1, Pallas kernels, shards(): pl.pallas_call(outer_kernel, grid=(steps,), out_shape=(jax.ShapeDtypeStru...  25.4 us

profile of v2, /device:TPU:0, one launch (start us, length us, event | category | flops | bytes accessed | tf_op | source)
XLA Modules:
  0.0 248.2 jit_solution(5204512516291411915)
XLA Ops:
  0.6 217.8 %power_iterations.1 = (bf16[1792,4096]{1,0:T(8,128)(2,1)}, bf16[192,1792]{1,0:T(8,128)(2,1)}, bf16[192,4096]{1,0:T(8,128)(2,1)}) custom-call(bf16[1,1792,4096]{2,1,0:T(8,128)(2,1)} %grad_ref.1, bf16[1,1792,4096]{2,1,0:T(8,128)(2,1)} %error_ref.1, f32[64,4096]{1,0:T(8,128)} %bitcast.8), custom_call_target="tpu_custom_call" | custom-call | tf_op jit(solution)/shard_map/power_iterations/pallas_call | solution.py:464
  218.5 1.1 dynamic-slice_bitcast_fusion
  219.5 0.1 copy.9
  219.7 1.4 copy.8
  221.1 0.2 pad_maximum_fusion.left_ref
  221.3 0.0 copy-start
  221.3 1.4 copy-done
  222.7 25.4 %outer_step.1 = (bf16[1,1792,4096]{2,1,0:T(8,128)(2,1)}, f32[448,4096]{1,0:T(8,128)}, f32[448,4096]{1,0:T(8,128)}) custom-call(bf16[1792,4096]{1,0:T(8,128)(2,1)} %get-tuple-element.6.combined_ref, bf16[14,160,192]{2,1,0:T(8,128)(2,1)S(1)} %pad_maximum_fusion.left_ref, bf16[192,4096]{1,0:T(8,128)(2,1)S(1)} %copy-done, f32[448,4096]{1,0:T(8,128)} %params_ref.1, ...), custom_call_target="tpu_custom_call" | custom-call | tf_op jit(solution)/shard_map/outer_step/pallas_call | solution.py:514
Async XLA Ops:
  221.3 1.4 copy-start

commit v3 on v2

--- a/solution.py
+++ b/solution.py
@@ -22,6 +22,12 @@
     high = value.astype(BF16)
     low = (value - high.astype(F32)).astype(BF16)
     return high, low
+
+
+def pair(twice):
+    high = twice.astype(BF16).astype(F32)
+    lane = lax.broadcasted_iota(jnp.int32, twice.shape, 1)
+    return jnp.where(lane < twice.shape[1] // 2, high, twice - high).astype(BF16)
 
 
 def bits_of(extent):
@@ -134,9 +140,7 @@
     @pl.loop(0, strips)
     def _(s):
         span = strip_span(s)
-        high, low = split(basis_ref[:, span])
-        basis_parts[0:rank, span] = high
-        basis_parts[rank:, span] = low
+        basis_parts[span, :] = pair(basis_ref[span, :])
 
     cut = (tiles + 1) // 2
     row_chunks = [(0, cut), (cut, tiles)] if tiles > 1 else [(0, 1)]
@@ -148,12 +152,7 @@
         return pl.ds(pl.multiple_of(t * tile, tile), tile)
 
     def sketch_part(t, cols):
-        both = lax.dot_general(
-            basis_parts[:, cols],
-            combined[tile_span(t), cols],
-            (((1,), (1,)), ((), ())),
-            preferred_element_type=F32,
-        )
+        both = jnp.dot(combined[tile_span(t), cols], basis_parts[cols, :], preferred_element_type=F32).T
         return both[0:rank] + both[rank:]
 
     def stream(begin, end):
@@ -181,16 +180,12 @@
     line = lax.broadcasted_iota(jnp.int32, (rank, 2 * rank), 0)
 
     def eliminate(begin, end):
-        def step(j, carry):
-            value = work[...]
-            row = work[pl.ds(j, 1), :]
-            column = jnp.sum(jnp.where(lane == j + rank, value, 0.0), axis=1, keepdims=True)
-            pivot = jnp.sum(jnp.where(lane[0:1] == j + rank, row, 0.0), axis=1, keepdims=True)
-            scale = jnp.where(line[:, 0:1] > j, column / pivot, 0.0)
-            work[...] = value - scale * row
-            return carry
-
-        lax.fori_loop(begin, end, step, 0)
+        value = work[...]
+        for j in range(begin, end):
+            column = jnp.broadcast_to(value[:, j + rank : j + rank + 1], value.shape)
+            row = value[j : j + 1] / column[j : j + 1]
+            value = value - jnp.where(line > j, column, 0.0) * row
+        work[...] = value
 
     core_peer, core = shard_peer(0)
     peer_a, bit_a = island_peer(0)
@@ -339,18 +334,19 @@
         last = len(flows) - 1
         for r, flow in enumerate(flows):
             resume(flow)
+            value = sketch[:, row_spans[r]]
+            square = lax.dot_general(
+                value,
+                jnp.concatenate([value, value], axis=0),
+                (((1,), (1,)), ((), ())),
+                precision=HIGH,
+                preferred_element_type=F32,
+            )
+            gram[...] = square if r == 0 else gram[...] + square
             if r < last:
                 project(r, 0)
                 project(r, 1)
 
-        value = sketch[...]
-        gram[...] = lax.dot_general(
-            value,
-            jnp.concatenate([value, value], axis=0),
-            (((1,), (1,)), ((), ())),
-            precision=HIGH,
-            preferred_element_type=F32,
-        )
         grams = gram_flow()
         resume(grams)
         halves = [factor_flow(0), factor_flow(1)]
@@ -395,11 +391,16 @@
 
         @pl.when(sweep == ITERS - 1)
         def _():
-            orthonormal = jnp.dot(inverse, sketch[...], precision=HIGH, preferred_element_type=F32)
-            high, low = split(orthonormal)
-            left_out[0:rank, :] = high
-            left_out[rank : 2 * rank, :] = high
-            left_out[2 * rank :, :] = low
+            thrice = lax.dot_general(
+                sketch[...].T,
+                jnp.concatenate([inverse] * 3, axis=0),
+                (((1,), (1,)), ((), ())),
+                precision=HIGH,
+                preferred_element_type=F32,
+            )
+            high = thrice.astype(BF16).astype(F32)
+            spot = lax.broadcasted_iota(jnp.int32, thrice.shape, 1)
+            left_out[...] = jnp.where(spot < 2 * rank, high, thrice - high).astype(BF16)
 
         while resume(halves[1]):
             pass
@@ -412,19 +413,27 @@
         return (value * (1.0 / jnp.sqrt(diagonal)))[:, 0:rank]
 
     def gathered(sweep, inverse, c):
-        @pl.loop(*chunk_strips[c])
-        def _(s):
-            span = strip_span(s)
-            basis = jnp.dot(inverse, projected_all[:, span], precision=HIGH, preferred_element_type=F32)
-
-            @pl.when(sweep < ITERS - 1)
-            def _():
-                high, low = split(basis)
-                basis_parts[0:rank, span] = high
-                basis_parts[rank:, span] = low
-
-            @pl.when(sweep == ITERS - 1)
-            def _():
+        @pl.when(sweep < ITERS - 1)
+        def _():
+            weight_high, weight_low = split(jnp.concatenate([inverse, inverse], axis=0))
+
+            @pl.loop(*chunk_strips[c])
+            def _(s):
+                span = strip_span(s)
+                high, low = split(projected_all[:, span].T)
+
+                def product(one, two):
+                    return lax.dot_general(one, two, (((1,), (1,)), ((), ())), preferred_element_type=F32)
+
+                twice = product(high, weight_high) + (product(high, weight_low) + product(low, weight_high))
+                basis_parts[span, :] = pair(twice)
+
+        @pl.when(sweep == ITERS - 1)
+        def _():
+            @pl.loop(*chunk_strips[c])
+            def _(s):
+                span = strip_span(s)
+                basis = jnp.dot(inverse, projected_all[:, span], precision=HIGH, preferred_element_type=F32)
                 high, low = split(basis * (1.0 / islands))
                 right_out[0:rank, span] = high
                 right_out[rank : 2 * rank, span] = low
@@ -436,8 +445,14 @@
 
 
 def outer_kernel(combined_ref, left_ref, right_ref, params_ref, momentum_ref, error_out, params_out, momentum_out):
-    tall = combined_ref.shape[0]
-    approx = jnp.dot(left_ref[0], right_ref[...], preferred_element_type=F32)
+    tall, short = combined_ref.shape[0], params_ref.shape[0]
+    step = pl.program_id(0)
+    begin = (lax.axis_index("island") * pl.num_programs(0) + step) * short
+    left = jnp.concatenate(
+        [left_ref[pl.ds(pl.multiple_of(step * tall, tall), tall), :], left_ref[pl.ds(pl.multiple_of(begin, short), short), :]],
+        axis=0,
+    )
+    approx = jnp.dot(left, right_ref[...], preferred_element_type=F32)
     error_out[0] = (combined_ref[...].astype(F32) - approx[0:tall]).astype(BF16)
     own = approx[tall:]
     new_momentum = momentum_coef * momentum_ref[...] + own
@@ -446,8 +461,8 @@
 
 
 def steps_of(rows, quarter):
-    for steps in (14, 7, 4, 2):
-        if rows % (16 * steps) == 0 and quarter % (8 * steps) == 0:
+    for steps in (7, 4, 2):
+        if rows % (16 * steps) == 0 and quarter % (16 * steps) == 0:
             return steps
     return 1
 
@@ -465,7 +480,7 @@
         functools.partial(power_kernel, islands, shard_count),
         out_shape=(
             jax.ShapeDtypeStruct((rows, wide), BF16),
-            jax.ShapeDtypeStruct((3 * rank, rows), BF16),
+            jax.ShapeDtypeStruct((rows, 3 * rank), BF16),
             jax.ShapeDtypeStruct((3 * rank, wide), BF16),
         ),
         in_specs=[hbm, hbm, vmem],
@@ -474,7 +489,7 @@
             pltpu.VMEM((rows, wide), BF16),
             pltpu.VMEM((2, tile, wide), BF16),
             pltpu.VMEM((2, tile, wide), BF16),
-            pltpu.VMEM((2 * rank, wide), BF16),
+            pltpu.VMEM((wide, 2 * rank), BF16),
             pltpu.VMEM((rank, rows), F32),
             pltpu.VMEM((island_bits, rank, rows), F32),
             pltpu.VMEM((2 * rank, rows), BF16),
@@ -502,15 +517,10 @@
             collective_id=0, has_side_effects=True, vmem_limit_bytes=56 * 1024 * 1024
         ),
         name="power_iterations",
-    )(pseudo_grad, error_buffer, basis_init.T)
-
-    left = left.T
+    )(pseudo_grad, error_buffer, jnp.concatenate([basis_init, basis_init], axis=1))
+
     steps = steps_of(rows, quarter)
-    own_left = lax.dynamic_slice_in_dim(left, lax.axis_index("island") * quarter, quarter, 0)
     tall, short = rows // steps, quarter // steps
-    left = jnp.concatenate(
-        [left.reshape(steps, tall, 3 * rank), own_left.reshape(steps, short, 3 * rank)], axis=1
-    )
     new_error, new_params, new_momentum = pl.pallas_call(
         outer_kernel,
         grid=(steps,),
@@ -521,7 +531,7 @@
         ),
         in_specs=[
             pl.BlockSpec((tall, wide), lambda i: (i, 0)),
-            pl.BlockSpec((1, tall + short, 3 * rank), lambda i: (i, 0, 0)),
+            pl.BlockSpec((rows, 3 * rank), lambda i: (0, 0)),
             pl.BlockSpec((3 * rank, wide), lambda i: (0, 0)),
             pl.BlockSpec((short, wide), lambda i: (i, 0)),
             pl.BlockSpec((short, wide), lambda i: (i, 0)),

time: 249 us -> 255 us (1.024)
  Pallas kernels: 243 us -> 248 us
    pallas_call x1, Pallas kernels: 218 us -> 224 us  [shards(): pl.pallas_call(functools.partial(power_kernel, islands, shard_count), out...]
    unnamed x2 -> x5, local copies, waits for them, and re-layouts: 1.4 us -> 4.4 us
where the time goes in v3:
time: 255 us
  Pallas kernels  248 us (97%)
  local copies, waits for them, and re-layouts  4.4 us (2%)
    pallas_call x1, Pallas kernels, shards(): pl.pallas_call(functools.partial(power_kernel, islands, shard_count), out...  224 us
    pallas_call x1, Pallas kernels, shards(): pl.pallas_call(outer_kernel, grid=(steps,), out_shape=(jax.ShapeDtypeStru...  23.2 us

profile of v3, /device:TPU:0, one launch (start us, length us, event | category | flops | bytes accessed | tf_op | source)
XLA Modules:
  0.0 254.7 jit_solution(11341578155034061810)
XLA Ops:
  0.6 1.8 copy.8
  2.5 1.9 pad_maximum_fusion.basis_ref
  4.4 224.5 %power_iterations.1 = (bf16[1792,4096]{1,0:T(8,128)(2,1)}, bf16[1792,192]{1,0:T(8,128)(2,1)}, bf16[192,4096]{1,0:T(8,128)(2,1)}) custom-call(bf16[1,1792,4096]{2,1,0:T(8,128)(2,1)} %grad_ref.1, bf16[1,1792,4096]{2,1,0:T(8,128)(2,1)} %error_ref.1, f32[4096,128]{1,0:T(8,128)} %pad_maximum_fusion.basis_ref), custom_call_target="tpu_custom_call" | custom-call | tf_op jit(solution)/shard_map/power_iterations/pallas_call | solution.py:479
  228.9 0.0 copy-start
  228.9 1.4 copy-done
  230.3 0.0 copy-start.1
  230.3 1.2 copy-done.1
  231.5 23.2 %outer_step.1 = (bf16[1,1792,4096]{2,1,0:T(8,128)(2,1)}, f32[448,4096]{1,0:T(8,128)}, f32[448,4096]{1,0:T(8,128)}) custom-call(bf16[1792,4096]{1,0:T(8,128)(2,1)} %get-tuple-element.6.combined_ref, bf16[1792,192]{1,0:T(8,128)(2,1)S(1)} %copy-done.1, bf16[192,4096]{1,0:T(8,128)(2,1)S(1)} %copy-done, f32[448,4096]{1,0:T(8,128)} %params_ref.1, ...), custom_call_target="tpu_custom_call" | custom-call | tf_op jit(solution)/shard_map/outer_step/pallas_call | solution.py:524
Async XLA Ops:
  228.9 1.4 copy-start
  230.3 1.2 copy-start.1

commit v4 on v3

--- a/solution.py
+++ b/solution.py
@@ -22,12 +22,6 @@
     high = value.astype(BF16)
     low = (value - high.astype(F32)).astype(BF16)
     return high, low
-
-
-def pair(twice):
-    high = twice.astype(BF16).astype(F32)
-    lane = lax.broadcasted_iota(jnp.int32, twice.shape, 1)
-    return jnp.where(lane < twice.shape[1] // 2, high, twice - high).astype(BF16)
 
 
 def bits_of(extent):
@@ -140,7 +134,9 @@
     @pl.loop(0, strips)
     def _(s):
         span = strip_span(s)
-        basis_parts[span, :] = pair(basis_ref[span, :])
+        high, low = split(basis_ref[:, span])
+        basis_parts[0:rank, span] = high
+        basis_parts[rank:, span] = low
 
     cut = (tiles + 1) // 2
     row_chunks = [(0, cut), (cut, tiles)] if tiles > 1 else [(0, 1)]
@@ -152,7 +148,12 @@
         return pl.ds(pl.multiple_of(t * tile, tile), tile)
 
     def sketch_part(t, cols):
-        both = jnp.dot(combined[tile_span(t), cols], basis_parts[cols, :], preferred_element_type=F32).T
+        both = lax.dot_general(
+            basis_parts[:, cols],
+            combined[tile_span(t), cols],
+            (((1,), (1,)), ((), ())),
+            preferred_element_type=F32,
+        )
         return both[0:rank] + both[rank:]
 
     def stream(begin, end):
@@ -355,39 +356,38 @@
         more = resume(grams)
         project(last, 1)
         resume(halves[1])
-        at = 0
+        resume(halves[0])
         while more:
             more = resume(grams)
-            if at < 2:
-                resume(halves[at])
-                at += 1
-        while at < 2:
-            resume(halves[at])
-            at += 1
         work[...] = jnp.where(lane < rank, jnp.where(lane == line, 1.0, 0.0), gram[...])
 
-        left_stages = 6 + (shard_bits - 1 if shard_bits > 1 else -1)
-        slots = 2 * left_stages - 1
+        ahead = rank // 8
+        eliminate(0, ahead)
+        resume(halves[0])
+        slots = 2 * (6 + (shard_bits if shard_bits > 1 else 0) - 2)
         place = 0
         more = True
         while more:
-            for half in halves:
+            for half in (halves[1], halves[0]):
                 if place < slots:
-                    eliminate(rank * place // slots, rank * (place + 1) // slots)
+                    eliminate(
+                        ahead + (rank - ahead) * place // slots, ahead + (rank - ahead) * (place + 1) // slots
+                    )
                 place += 1
                 more = resume(half)
-                if not more:
-                    break
         if place < slots:
-            eliminate(rank * place // slots, rank)
+            eliminate(ahead + (rank - ahead) * place // slots, rank)
         inverse = inverse_factor()
         gathered(sweep, inverse, 0)
 
-        @pl.when(sweep < ITERS - 1)
-        def _():
-            @pl.loop(0, tiles)
-            def _(t):
-                sketch[:, tile_span(t)] = sketch_part(t, columns[0])
+        for begin, end in row_chunks:
+            resume(halves[1])
+
+            @pl.when(sweep < ITERS - 1)
+            def _():
+                @pl.loop(begin, end)
+                def _(t):
+                    sketch[:, tile_span(t)] = sketch_part(t, columns[0])
 
         @pl.when(sweep == ITERS - 1)
         def _():
@@ -415,18 +415,18 @@
     def gathered(sweep, inverse, c):
         @pl.when(sweep < ITERS - 1)
         def _():
-            weight_high, weight_low = split(jnp.concatenate([inverse, inverse], axis=0))
+            weight_high, weight_low = split(inverse)
+            weights = jnp.concatenate([weight_high, weight_low], axis=0)
 
             @pl.loop(*chunk_strips[c])
             def _(s):
                 span = strip_span(s)
-                high, low = split(projected_all[:, span].T)
-
-                def product(one, two):
-                    return lax.dot_general(one, two, (((1,), (1,)), ((), ())), preferred_element_type=F32)
-
-                twice = product(high, weight_high) + (product(high, weight_low) + product(low, weight_high))
-                basis_parts[span, :] = pair(twice)
+                high, low = split(projected_all[:, span])
+                both = jnp.dot(weights, high, preferred_element_type=F32)
+                small = both[rank:] + jnp.dot(weight_high, low, preferred_element_type=F32)
+                high, low = split(both[0:rank] + small)
+                basis_parts[0:rank, span] = high
+                basis_parts[rank:, span] = low
 
         @pl.when(sweep == ITERS - 1)
         def _():
@@ -489,7 +489,7 @@
             pltpu.VMEM((rows, wide), BF16),
             pltpu.VMEM((2, tile, wide), BF16),
             pltpu.VMEM((2, tile, wide), BF16),
-            pltpu.VMEM((wide, 2 * rank), BF16),
+            pltpu.VMEM((2 * rank, wide), BF16),
             pltpu.VMEM((rank, rows), F32),
             pltpu.VMEM((island_bits, rank, rows), F32),
             pltpu.VMEM((2 * rank, rows), BF16),
@@ -517,7 +517,7 @@
             collective_id=0, has_side_effects=True, vmem_limit_bytes=56 * 1024 * 1024
         ),
         name="power_iterations",
-    )(pseudo_grad, error_buffer, jnp.concatenate([basis_init, basis_init], axis=1))
+    )(pseudo_grad, error_buffer, basis_init.T)
 
     steps = steps_of(rows, quarter)
     tall, short = rows // steps, quarter // steps

time: 255 us -> 252 us (0.988)
  no operation moved by 1% of the time
where the time goes in v4:
time: 252 us; the launch traced here: 251 us
  Pallas kernels  248 us (98%)
  local copies, waits for them, and re-layouts  2.58 us (1%)
    pallas_call x1, Pallas kernels, shards(): pl.pallas_call(functools.partial(power_kernel, islands, shard_count), out...  225 us
    pallas_call x1, Pallas kernels, shards(): pl.pallas_call(outer_kernel, grid=(steps,), out_shape=(jax.ShapeDtypeStru...  23.2 us

profile of v4, /device:TPU:0, one launch (start us, length us, event | category | flops | bytes accessed | tf_op | source)
XLA Modules:
  0.0 251.5 jit_solution(253645009611642224)
XLA Ops:
  0.6 225.0 %power_iterations.1 = (bf16[1792,4096]{1,0:T(8,128)(2,1)}, bf16[1792,192]{1,0:T(8,128)(2,1)}, bf16[192,4096]{1,0:T(8,128)(2,1)}) custom-call(bf16[1,1792,4096]{2,1,0:T(8,128)(2,1)} %grad_ref.1, bf16[1,1792,4096]{2,1,0:T(8,128)(2,1)} %error_ref.1, f32[64,4096]{1,0:T(8,128)} %bitcast.1), custom_call_target="tpu_custom_call" | custom-call | tf_op jit(solution)/shard_map/power_iterations/pallas_call | solution.py:479
  225.7 0.0 copy-start
  225.7 1.4 copy-done
  227.1 0.0 copy-start.1
  227.1 1.2 copy-done.1
  228.3 23.2 %outer_step.1 = (bf16[1,1792,4096]{2,1,0:T(8,128)(2,1)}, f32[448,4096]{1,0:T(8,128)}, f32[448,4096]{1,0:T(8,128)}) custom-call(bf16[1792,4096]{1,0:T(8,128)(2,1)} %get-tuple-element.6.combined_ref, bf16[1792,192]{1,0:T(8,128)(2,1)S(1)} %copy-done.1, bf16[192,4096]{1,0:T(8,128)(2,1)S(1)} %copy-done, f32[448,4096]{1,0:T(8,128)} %params_ref.1, ...), custom_call_target="tpu_custom_call" | custom-call | tf_op jit(solution)/shard_map/outer_step/pallas_call | solution.py:524
Async XLA Ops:
  225.7 1.4 copy-start
  227.1 1.2 copy-start.1
